TPU v7x, 512 devices: a whole 4x8x8 slice. The times are simulated.
512 devices in a mesh: row: 32 (over z_hi, x, core), col: 16 (over y, z_lo).
Axes of the slice: x: 4, y: 8, z: 8 (z_hi: 4, z_lo: 2; z = z_hi * 2 + z_lo), core: 2. Of those that a mesh axis runs over, the one named last changes fastest.
Arguments:
- pair: float32 [384, 384, 128], P('row', 'col'), may hold values from -6 to 6
- cotangent: float32 [384, 384, 128], P('row', 'col'), may hold values from -6 to 6
- norm_gain: float32 [128], replicated, may hold values from 0.5 to 1.5
- gate_a: float32 [128, 128], replicated, may hold values from -0.5 to 0.5
- proj_a: float32 [128, 128], replicated, may hold values from -0.5 to 0.5
- gate_b: float32 [128, 128], replicated, may hold values from -0.5 to 0.5
- proj_b: float32 [128, 128], replicated, may hold values from -0.5 to 0.5
- mix_gain: float32 [128], replicated, may hold values from 0.5 to 1.5
- out_gate: float32 [128, 128], replicated, may hold values from -0.5 to 0.5
- out_proj: float32 [128, 128], replicated, may hold values from -0.5 to 0.5
Outputs:
- pair_grad: float32 [384, 384, 128], P('row', 'col')
All inputs are finite; a program needn't handle non-finite values.
Results may differ from a plain program's by a relative error of at most 0.000084.
Values sent between devices are 32-bit elements; how exact they have to be, the bound alone decides.
A program may use at most 64 MiB of HBM per device.

v0:
```python
import jax
import jax.numpy as jnp
from jax import lax
from jax.experimental import pallas as pl
from jax.experimental.pallas import tpu as pltpu
from jax.sharding import PartitionSpec as P

MESH = pl.DeviceIdType.MESH
F32 = jnp.float32
NN = (((1,), (0,)), ((), ()))
NT = (((1,), (1,)), ((), ()))


def split(values):
    high = values.astype(jnp.bfloat16)
    return high, (values - high.astype(F32)).astype(jnp.bfloat16)


def product(a, b, dims=NN):
    def one(x, y):
        return lax.dot_general(x, y, dims, preferred_element_type=F32)

    return one(a[0], b[1]) + one(a[1], b[0]) + one(a[0], b[0])


def column(ref):
    return jnp.broadcast_to(ref[...], (8, 128)).T[:, 0:1]


def mean0(values):
    return jnp.mean(values, axis=0, keepdims=True)


def kernel(pair_ref, cot_ref, norm_gain_ref, gate_a_ref, proj_a_ref, gate_b_ref, proj_b_ref, mix_gain_ref,
           out_gate_ref, out_proj_ref, out_ref,
           s1, r1, left_x, right_t, right_x, s2, r2, s3, r3, grad_x, dl_out, dl_in, dl_own, dr_full, dr_t, dr_in,
           s4, r4, keep, stats, send_sem, recv_sem, hop):
    row = lax.axis_index("row")
    col = lax.axis_index("col")
    core = row % 2
    low = (row // 2) % 2
    part = row // 4
    quarter = row % 4
    mine = col * 8 + part
    x_peer = (row + 2 - 4 * low, col)
    core_peer = (row + 1 - 2 * core, col)

    barrier = pltpu.get_barrier_semaphore()

    def signal(sem, device):
        pl.semaphore_signal(sem, inc=1, device_id=device, device_id_type=MESH)

    def greet_col(k, carry):
        signal(barrier, (row, (col + k) % 16))
        return carry

    def greet_row(k, carry):
        signal(barrier, ((row + 4 * k) % 32, col))
        return carry

    def pass_on(k, carry):
        signal(hop, ((row + 4 * k) % 32, col))
        return carry

    lax.fori_loop(1, 16, greet_col, 0)
    lax.fori_loop(1, 8, greet_row, 0)
    signal(barrier, x_peer)
    signal(barrier, core_peer)

    def remote(src, dst, phase, device):
        return pltpu.make_async_remote_copy(
            src_ref=src, dst_ref=dst, send_sem=send_sem.at[phase], recv_sem=recv_sem.at[phase],
            device_id=device, device_id_type=MESH)

    def wait(ref, sem):
        pltpu.make_async_copy(ref, ref, sem).wait()

    ng = column(norm_gain_ref)
    mg = column(mix_gain_ref)
    pair = pair_ref[...].reshape(288, 128).T
    centred = pair - mean0(pair)
    inverse = lax.rsqrt(mean0(centred * centred) + 1e-05)
    plain = centred * inverse
    normed = split(plain * ng)
    weights = jnp.concatenate(
        [gate_a_ref[...], proj_a_ref[...], gate_b_ref[...], proj_b_ref[...], out_gate_ref[...]], axis=1)
    projected = product(split(weights.T), normed)
    left_gate = jax.nn.sigmoid(projected[0:128])
    left_value = projected[128:256]
    right_gate = jax.nn.sigmoid(projected[256:384])
    right_value = projected[384:512]
    s1[:, 0, :] = jnp.concatenate([left_gate * left_value, right_gate * right_value], axis=1)

    pl.semaphore_wait(barrier, 24)
    lax.fori_loop(1, 8, pass_on, 0)
    pl.semaphore_wait(hop, 7)

    def send_edges(k, carry):
        q = (mine + k) % 128
        remote(s1.at[q], r1.at[mine], 0, ((q % 8) * 4 + quarter, q // 8)).start()
        return carry

    lax.fori_loop(1, 128, send_edges, 0)
    pltpu.make_async_copy(s1.at[mine], r1.at[mine], recv_sem.at[0]).start()

    keep[0] = plain
    keep[1] = left_gate
    keep[2] = left_value * left_gate * (1.0 - left_gate)
    keep[3] = right_gate
    keep[4] = right_value * right_gate * (1.0 - right_gate)
    out_sig = jax.nn.sigmoid(projected[512:640])
    grad_value = cot_ref[...].reshape(288, 128).T * out_sig
    keep[5] = grad_value * (1.0 - out_sig)
    out_proj = out_proj_ref[...]
    scaled = product(split(out_proj), split(grad_value)) * mg
    keep[6] = scaled - mean0(scaled)
    keep[7] = scaled
    stats[0:1] = inverse

    wait(r1, recv_sem.at[0])
    for n in range(12):
        left_x[low, 8 * n:8 * n + 8, :] = jnp.concatenate(
            [r1[8 * c:8 * c + 8, 0, 24 * n:24 * n + 24] for c in range(16)], axis=1)
    send_left = remote(left_x.at[low], left_x.at[low], 1, x_peer)
    send_left.start()
    for n in range(12):
        right_t[core, 8 * n:8 * n + 8, :] = jnp.concatenate(
            [r1[8 * c:8 * c + 8, 0, 24 * n + 288:24 * n + 312] for c in range(16)], axis=1)
    send_right = remote(right_t.at[core], right_t.at[core], 2, core_peer)
    send_right.start()
    send_right.wait_recv()
    for side in range(2):
        for n in range(12):
            for t in range(3):
                right_x[t, pl.ds(12 * side + n, 8, stride=24), :] = right_t[
                    side, 8 * n:8 * n + 8, 128 * t:128 * t + 128]

    def right_all():
        return split(jnp.concatenate([right_x[t] for t in range(3)], axis=1))

    right = right_all()

    same = (col % 2) == low
    place = (col // 2) * 8 + part

    def mix(half):
        mixed = product(split(left_x[half]), right, NT)
        for b in range(8):
            s2[pl.ds(half * 64 + 8 * b, 8), 0, :] = jnp.concatenate(
                [mixed[8 * n:8 * n + 8, 24 * b:24 * b + 24] for n in range(12)], axis=1)

    def mixed_copy(half, q):
        target = ((q % 8) * 4 + half * 2 + core, (q // 8) * 2 + low)
        return remote(s2.at[half * 64 + q], r2.at[mine], 3, target)

    mix(low)

    def send_mixed_own(k, carry):
        mixed_copy(low, (place + k) % 64).start()
        return carry

    lax.fori_loop(1, 64, send_mixed_own, 0)

    @pl.when(same)
    def _():
        pltpu.make_async_copy(s2.at[low * 64 + place], r2.at[mine], recv_sem.at[3]).start()

    @pl.when(jnp.logical_not(same))
    def _():
        mixed_copy(low, place).start()

    send_left.wait_recv()
    mix(1 - low)

    def send_mixed_other(k, carry):
        mixed_copy(1 - low, (place + k) % 64).start()
        return carry

    lax.fori_loop(0, 64, send_mixed_other, 0)

    wait(r2, recv_sem.at[3])
    mixed = r2[:, 0, :]
    mixed = mixed - mean0(mixed)
    mixed_inverse = lax.rsqrt(mean0(mixed * mixed) + 1e-05)
    mixed_plain = mixed * mixed_inverse
    second = mean0(keep[7] * mixed_plain)
    s3[:, 0, :] = mixed_inverse * (keep[6] - mixed_plain * second)

    source = (col % 2) * 2 + core
    slot = low * 64 + (col // 2) * 8 + part

    def grad_copy(q):
        return remote(s3.at[q], r3.at[slot], 4, ((q % 8) * 4 + source, q // 8))

    def send_grad(k, carry):
        grad_copy((mine + k) % 128).start()
        return carry

    lax.fori_loop(1, 128, send_grad, 0)

    @pl.when(same)
    def _():
        pltpu.make_async_copy(s3.at[mine], r3.at[slot], recv_sem.at[4]).start()

    @pl.when(jnp.logical_not(same))
    def _():
        grad_copy(mine).start()

    out_value = product(split(out_proj.T), split(mixed_plain * mg))
    keep[6] = product(split(out_gate_ref[...]), split(keep[5] * out_value))

    wait(r3, recv_sem.at[4])
    for half in range(2):
        for n in range(12):
            grad_x[half, 8 * n:8 * n + 8, :] = jnp.concatenate(
                [r3[64 * half + 8 * b:64 * half + 8 * b + 8, 0, 24 * n:24 * n + 24] for b in range(8)], axis=1)
    right = right_all()
    dl_out[...] = product(split(grad_x[1 - low]), right)
    send_dl = remote(dl_out, dl_in, 5, x_peer)
    send_dl.start()
    grad_t = grad_x[...].reshape(192, 192).T
    dr = product(split(grad_t), split(left_x[...].reshape(192, 384)))
    for t in range(3):
        dr_full[t] = dr[:, 128 * t:128 * t + 128]
    for side in range(2):
        for n in range(12):
            for t in range(3):
                dr_t[side, 8 * n:8 * n + 8, 128 * t:128 * t + 128] = dr_full[
                    t, pl.ds(12 * side + n, 8, stride=24), :]
    send_dr = remote(dr_t.at[1 - core], dr_in, 6, core_peer)
    send_dr.start()
    dl_own[...] = product(split(grad_x[low]), right)
    send_dr.wait_recv()
    send_dl.wait_recv()
    dl = dl_own[...] + dl_in[...]
    dr = dr_t[core] + dr_in[...]
    for c in range(16):
        s4[8 * c:8 * c + 8, 0, :] = jnp.concatenate(
            [x[8 * n:8 * n + 8, 24 * c:24 * c + 24] for x in (dl, dr) for n in range(12)], axis=1)

    def send_back(k, carry):
        q = (mine + k) % 128
        remote(s4.at[q], r4.at[mine], 7, ((q % 8) * 4 + quarter, q // 8)).start()
        return carry

    lax.fori_loop(1, 128, send_back, 0)
    pltpu.make_async_copy(s4.at[mine], r4.at[mine], recv_sem.at[7]).start()

    wait(r4, recv_sem.at[7])
    dl = r4[:, 0, 0:288]
    dr = r4[:, 0, 288:576]
    stacked = jnp.concatenate([dl * keep[2], dl * keep[1], dr * keep[4], dr * keep[3]], axis=0)
    weights = jnp.concatenate([gate_a_ref[...], proj_a_ref[...], gate_b_ref[...], proj_b_ref[...]], axis=1)
    grad = (product(split(weights), split(stacked)) + keep[6]) * ng
    plain = keep[0]
    grad = stats[0:1] * (grad - mean0(grad) - plain * mean0(grad * plain))
    out_ref[...] = grad.T.reshape(12, 24, 128)

    send_left.wait_send()
    send_right.wait_send()
    send_dl.wait_send()
    send_dr.wait_send()
    wait(s1.at[pl.ds(0, 127)], send_sem.at[0])
    wait(s4.at[pl.ds(0, 127)], send_sem.at[7])
    wait(s2.at[pl.ds(0, 127)], send_sem.at[3])
    wait(s3.at[pl.ds(0, 127)], send_sem.at[4])

    @pl.when(jnp.logical_not(same))
    def _():
        wait(s2.at[0], send_sem.at[3])
        wait(s3.at[0], send_sem.at[4])


def local(pair, cotangent, norm_gain, gate_a, proj_a, gate_b, proj_b, mix_gain, out_gate, out_proj):
    def vmem(*shape):
        return pltpu.VMEM(shape, F32)

    return pl.pallas_call(
        kernel,
        out_shape=jax.ShapeDtypeStruct(pair.shape, F32),
        in_specs=[pl.BlockSpec(memory_space=pltpu.VMEM)] * 10,
        out_specs=pl.BlockSpec(memory_space=pltpu.VMEM),
        scratch_shapes=[
            vmem(128, 1, 576), vmem(128, 1, 576),
            vmem(2, 96, 384), vmem(2, 96, 384), vmem(3, 192, 128),
            vmem(128, 1, 288), vmem(128, 1, 288),
            vmem(128, 1, 288), vmem(128, 1, 288),
            vmem(2, 96, 192),
            vmem(96, 384), vmem(96, 384), vmem(96, 384),
            vmem(3, 192, 128), vmem(2, 96, 384), vmem(96, 384),
            vmem(128, 1, 576), vmem(128, 1, 576),
            vmem(8, 128, 288), vmem(8, 288),
            pltpu.SemaphoreType.DMA((8,)), pltpu.SemaphoreType.DMA((8,)), pltpu.SemaphoreType.REGULAR,
        ],
        compiler_params=pltpu.CompilerParams(
            collective_id=0, has_side_effects=True, vmem_limit_bytes=48 * 1024 * 1024),
    )(pair, cotangent, norm_gain.reshape(1, 128), gate_a, proj_a, gate_b, proj_b, mix_gain.reshape(1, 128),
      out_gate, out_proj)


def solution(mesh):
    placed = (P("row", "col", None), P("row", "col", None), P(), P(), P(), P(), P(), P(), P(), P())
    return jax.shard_map(
        local, mesh=mesh, in_specs=placed, out_specs=P("row", "col", None), check_vma=False)
```

profile of v0, /device:TPU:16, one launch (start us, length us, event | category | flops | bytes accessed | tf_op | source)
XLA Modules:
  0.0 84.2 jit_solution(11579536938760022881)
XLA Ops:
  0.0 0.0 copy-start.8
  0.0 0.0 copy-start.9
  0.0 0.7 copy-done.8
  0.7 0.0 copy-done.9
  0.7 0.0 copy-start
  0.7 0.9 %copy-done = f32[12,24,128]{2,1,0:T(8,128)S(1)} copy-done((f32[12,24,128]{2,1,0:T(8,128)S(1)}, f32[12,24,128]{2,1,0:T(8,128)}, u32[]{:S(2)}) %copy-start) | copy-done | bytes 147480
  1.6 0.0 copy-start.1
  1.6 0.9 %copy-done.1 = f32[12,24,128]{2,1,0:T(8,128)S(1)} copy-done((f32[12,24,128]{2,1,0:T(8,128)S(1)}, f32[12,24,128]{2,1,0:T(8,128)}, u32[]{:S(2)}) %copy-start.1) | copy-done | bytes 147480
  2.5 0.0 copy-start.2
  2.5 0.8 copy-done.2
  3.3 0.0 copy-start.3
  3.3 0.8 copy-done.3
  4.2 0.0 copy-start.4
  4.2 0.8 copy-done.4
  5.0 0.0 copy-start.5
  5.0 0.8 copy-done.5
  5.9 0.0 copy-start.6
  5.9 0.8 copy-done.6
  6.7 0.0 copy-start.7
  6.7 0.8 copy-done.7
  7.5 76.0 %shard_map.100 = f32[12,24,128]{2,1,0:T(8,128)S(1)} custom-call(f32[12,24,128]{2,1,0:T(8,128)S(1)} %copy-done, f32[12,24,128]{2,1,0:T(8,128)S(1)} %copy-done.1, f32[1,128]{1,0:T(1,128)S(1)} %bitcast.2, f32[128,128]{1,0:T(8,128)S(1)} %copy-done.2, f32[128,128]{1,0:T(8,128)S(1)} %copy-done.3, f32[128,128]{1,0:T(8,128)S(1)} %copy-done.4, ...), custom_call_target="tpu_custom_call" | custom-call | tf_op jit(solution)/shard_map/pallas_call | solution.py:278
  83.5 0.7 copy.12
Async XLA Ops:
  0.0 0.7 copy-start.8
  0.0 0.7 copy-start.9
  0.7 0.9 %copy-start = (f32[12,24,128]{2,1,0:T(8,128)S(1)}, f32[12,24,128]{2,1,0:T(8,128)}, u32[]{:S(2)}) copy-start(f32[12,24,128]{2,1,0:T(8,128)} %pair_ref.1) | copy-start | bytes 442372
  1.6 0.9 %copy-start.1 = (f32[12,24,128]{2,1,0:T(8,128)S(1)}, f32[12,24,128]{2,1,0:T(8,128)}, u32[]{:S(2)}) copy-start(f32[12,24,128]{2,1,0:T(8,128)} %cot_ref.1) | copy-start | bytes 442372
  2.5 0.8 copy-start.2
  3.3 0.8 copy-start.3
  4.2 0.8 copy-start.4
  5.0 0.8 copy-start.5
  5.9 0.8 copy-start.6
  6.7 0.8 copy-start.7
where the time goes:
time: 84.6 us; the launch traced here: 84.2 us
  Pallas kernels  76 us (90%)
  local copies, waits for them, and re-layouts  8.19 us (10%)
    pallas_call x1, Pallas kernels, local(): pl.pallas_call(kernel, out_shape=jax.ShapeDtypeStruct(pair.shape, F32), i...  76 us
    unnamed x21, local copies, waits for them, and re-layouts  8.19 us

commit v1 on v0

--- a/solution.py
+++ b/solution.py
@@ -23,49 +23,79 @@
     return one(a[0], b[1]) + one(a[1], b[0]) + one(a[0], b[0])
 
 
-def column(ref):
-    return jnp.broadcast_to(ref[...], (8, 128)).T[:, 0:1]
+def column(row):
+    return jnp.broadcast_to(row, (8, 128)).T[:, 0:1]
 
 
 def mean0(values):
     return jnp.mean(values, axis=0, keepdims=True)
 
 
-def kernel(pair_ref, cot_ref, norm_gain_ref, gate_a_ref, proj_a_ref, gate_b_ref, proj_b_ref, mix_gain_ref,
-           out_gate_ref, out_proj_ref, out_ref,
-           s1, r1, left_x, right_t, right_x, s2, r2, s3, r3, grad_x, dl_out, dl_in, dl_own, dr_full, dr_t, dr_in,
-           s4, r4, keep, stats, send_sem, recv_sem, hop):
+def kernel(pair_hbm, cot_hbm, norm_gain_hbm, gate_a_hbm, proj_a_hbm, gate_b_hbm, proj_b_hbm, mix_gain_hbm,
+           out_gate_hbm, out_proj_hbm, out_ref,
+           pair_ref, cot_ref, gains, weights_ref, out_proj_ref, s1, r1, left_x, right_t, right_x, s2, r2, s3, r3, grad_x, dl_out, dl_in, dl_own, dr_full, dr_t, dr_in,
+           s4, r4, keep, stats, load_sem, send_sem, recv_sem):
     row = lax.axis_index("row")
     col = lax.axis_index("col")
-    core = row % 2
-    low = (row // 2) % 2
-    part = row // 4
-    quarter = row % 4
+    core = lax.rem(row, 2)
+    low = lax.rem(lax.div(row, 2), 2)
+    part = lax.div(row, 4)
+    quarter = lax.rem(row, 4)
     mine = col * 8 + part
     x_peer = (row + 2 - 4 * low, col)
     core_peer = (row + 1 - 2 * core, col)
 
+    loads = [
+        pltpu.make_async_copy(source, target, load_sem.at[i])
+        for i, (source, target) in enumerate([
+            (pair_hbm, pair_ref),
+            (norm_gain_hbm, gains.at[0]),
+            (gate_a_hbm, weights_ref.at[:, pl.ds(0, 128)]),
+            (proj_a_hbm, weights_ref.at[:, pl.ds(128, 128)]),
+            (gate_b_hbm, weights_ref.at[:, pl.ds(256, 128)]),
+            (proj_b_hbm, weights_ref.at[:, pl.ds(384, 128)]),
+            (out_gate_hbm, weights_ref.at[:, pl.ds(512, 128)]),
+            (mix_gain_hbm, gains.at[1]),
+            (cot_hbm, cot_ref),
+            (out_proj_hbm, out_proj_ref),
+        ])
+    ]
+    for load in loads:
+        load.start()
+
     barrier = pltpu.get_barrier_semaphore()
 
-    def signal(sem, device):
-        pl.semaphore_signal(sem, inc=1, device_id=device, device_id_type=MESH)
-
-    def greet_col(k, carry):
-        signal(barrier, (row, (col + k) % 16))
-        return carry
-
-    def greet_row(k, carry):
-        signal(barrier, ((row + 4 * k) % 32, col))
-        return carry
-
-    def pass_on(k, carry):
-        signal(hop, ((row + 4 * k) % 32, col))
-        return carry
-
-    lax.fori_loop(1, 16, greet_col, 0)
-    lax.fori_loop(1, 8, greet_row, 0)
-    signal(barrier, x_peer)
-    signal(barrier, core_peer)
+    def greet(device):
+        pl.semaphore_signal(barrier, inc=1, device_id=device, device_id_type=MESH)
+
+    def mod(value, size):
+        return lax.rem(value, size)
+
+    y_here, z_here = lax.div(col, 2), lax.div(row, 8) * 2 + lax.rem(col, 2)
+    z_all = [mod(z_here + t, 8) for t in range(8)]
+    z_place = [lax.div(z, 2) * 2 for z in z_all]
+    z_column = [lax.rem(z, 2) for z in z_all]
+    x_place = [lax.rem(part + t, 2) for t in range(2)]
+
+    def y_far(step):
+        return mod(y_here + 4 + lax.div(step + 1, 2) * (1 - 2 * mod(step, 2)), 8) * 2
+
+    inner = sorted(((z, x) for z in range(8) for x in range(2)), key=lambda o: -min(o[0], 8 - o[0]) - 2 * o[1])
+
+    def each_channel(visit):
+        def one(step, carry):
+            column = y_far(step)
+            for z, x in inner:
+                visit(z_place[z] + x_place[x], column + z_column[z])
+            return carry
+
+        lax.fori_loop(0, 7, one, 0)
+        for z, x in inner[:-1]:
+            visit(z_place[z] + x_place[x], y_here * 2 + z_column[z])
+
+    greet(x_peer)
+    greet(core_peer)
+    each_channel(lambda place, column: greet((place * 4 + quarter, column)))
 
     def remote(src, dst, phase, device):
         return pltpu.make_async_remote_copy(
@@ -75,32 +105,29 @@
     def wait(ref, sem):
         pltpu.make_async_copy(ref, ref, sem).wait()
 
-    ng = column(norm_gain_ref)
-    mg = column(mix_gain_ref)
+    for load in loads[0:2]:
+        load.wait()
+    ng = column(gains[0])
     pair = pair_ref[...].reshape(288, 128).T
     centred = pair - mean0(pair)
     inverse = lax.rsqrt(mean0(centred * centred) + 1e-05)
     plain = centred * inverse
     normed = split(plain * ng)
-    weights = jnp.concatenate(
-        [gate_a_ref[...], proj_a_ref[...], gate_b_ref[...], proj_b_ref[...], out_gate_ref[...]], axis=1)
-    projected = product(split(weights.T), normed)
+    for load in loads[2:7]:
+        load.wait()
+    projected = product(split(weights_ref[...].T), normed)
     left_gate = jax.nn.sigmoid(projected[0:128])
     left_value = projected[128:256]
     right_gate = jax.nn.sigmoid(projected[256:384])
     right_value = projected[384:512]
     s1[:, 0, :] = jnp.concatenate([left_gate * left_value, right_gate * right_value], axis=1)
 
-    pl.semaphore_wait(barrier, 24)
-    lax.fori_loop(1, 8, pass_on, 0)
-    pl.semaphore_wait(hop, 7)
-
-    def send_edges(k, carry):
-        q = (mine + k) % 128
-        remote(s1.at[q], r1.at[mine], 0, ((q % 8) * 4 + quarter, q // 8)).start()
-        return carry
-
-    lax.fori_loop(1, 128, send_edges, 0)
+    pl.semaphore_wait(barrier, 129)
+
+    def send_edges(place, column):
+        remote(s1.at[column * 8 + place], r1.at[mine], 0, (place * 4 + quarter, column)).start()
+
+    each_channel(send_edges)
     pltpu.make_async_copy(s1.at[mine], r1.at[mine], recv_sem.at[0]).start()
 
     keep[0] = plain
@@ -108,6 +135,9 @@
     keep[2] = left_value * left_gate * (1.0 - left_gate)
     keep[3] = right_gate
     keep[4] = right_value * right_gate * (1.0 - right_gate)
+    for load in loads[7:10]:
+        load.wait()
+    mg = column(gains[1])
     out_sig = jax.nn.sigmoid(projected[512:640])
     grad_value = cot_ref[...].reshape(288, 128).T * out_sig
     keep[5] = grad_value * (1.0 - out_sig)
@@ -140,8 +170,8 @@
 
     right = right_all()
 
-    same = (col % 2) == low
-    place = (col // 2) * 8 + part
+    same = lax.rem(col, 2) == low
+    slot = low * 64 + y_here * 8 + part
 
     def mix(half):
         mixed = product(split(left_x[half]), right, NT)
@@ -149,34 +179,40 @@
             s2[pl.ds(half * 64 + 8 * b, 8), 0, :] = jnp.concatenate(
                 [mixed[8 * n:8 * n + 8, 24 * b:24 * b + 24] for n in range(12)], axis=1)
 
-    def mixed_copy(half, q):
-        target = ((q % 8) * 4 + half * 2 + core, (q // 8) * 2 + low)
-        return remote(s2.at[half * 64 + q], r2.at[mine], 3, target)
+    def mixed_copy(half, column, place):
+        return remote(s2.at[half * 64 + lax.div(column, 2) * 8 + place], r2.at[mine], 3,
+                      (place * 4 + half * 2 + core, column + low))
+
+    z_half = [lax.rem(lax.div(row, 8) + t, 4) * 2 for t in range(4)]
+    inner_half = ((2, 1), (2, 0), (1, 1), (3, 1), (1, 0), (3, 0), (0, 1), (0, 0))
+
+    def send_mixed(half, last):
+        def one(step, carry):
+            column = y_far(step)
+            for z, x in inner_half:
+                mixed_copy(half, column, z_half[z] + x_place[x]).start()
+            return carry
+
+        lax.fori_loop(0, 7, one, 0)
+        for z, x in inner_half[:last]:
+            mixed_copy(half, y_here * 2, z_half[z] + x_place[x]).start()
 
     mix(low)
 
-    def send_mixed_own(k, carry):
-        mixed_copy(low, (place + k) % 64).start()
-        return carry
-
-    lax.fori_loop(1, 64, send_mixed_own, 0)
+    send_mixed(low, 7)
 
     @pl.when(same)
     def _():
-        pltpu.make_async_copy(s2.at[low * 64 + place], r2.at[mine], recv_sem.at[3]).start()
+        pltpu.make_async_copy(s2.at[slot], r2.at[mine], recv_sem.at[3]).start()
 
     @pl.when(jnp.logical_not(same))
     def _():
-        mixed_copy(low, place).start()
+        mixed_copy(low, y_here * 2, part).start()
 
     send_left.wait_recv()
     mix(1 - low)
 
-    def send_mixed_other(k, carry):
-        mixed_copy(1 - low, (place + k) % 64).start()
-        return carry
-
-    lax.fori_loop(0, 64, send_mixed_other, 0)
+    send_mixed(1 - low, 8)
 
     wait(r2, recv_sem.at[3])
     mixed = r2[:, 0, :]
@@ -186,17 +222,12 @@
     second = mean0(keep[7] * mixed_plain)
     s3[:, 0, :] = mixed_inverse * (keep[6] - mixed_plain * second)
 
-    source = (col % 2) * 2 + core
-    slot = low * 64 + (col // 2) * 8 + part
-
-    def grad_copy(q):
-        return remote(s3.at[q], r3.at[slot], 4, ((q % 8) * 4 + source, q // 8))
-
-    def send_grad(k, carry):
-        grad_copy((mine + k) % 128).start()
-        return carry
-
-    lax.fori_loop(1, 128, send_grad, 0)
+    source = lax.rem(col, 2) * 2 + core
+
+    def grad_copy(place, column):
+        return remote(s3.at[column * 8 + place], r3.at[slot], 4, (place * 4 + source, column))
+
+    each_channel(lambda place, column: grad_copy(place, column).start())
 
     @pl.when(same)
     def _():
@@ -204,10 +235,10 @@
 
     @pl.when(jnp.logical_not(same))
     def _():
-        grad_copy(mine).start()
+        grad_copy(part, col).start()
 
     out_value = product(split(out_proj.T), split(mixed_plain * mg))
-    keep[6] = product(split(out_gate_ref[...]), split(keep[5] * out_value))
+    keep[6] = product(split(weights_ref[:, 512:640]), split(keep[5] * out_value))
 
     wait(r3, recv_sem.at[4])
     for half in range(2):
@@ -238,20 +269,17 @@
         s4[8 * c:8 * c + 8, 0, :] = jnp.concatenate(
             [x[8 * n:8 * n + 8, 24 * c:24 * c + 24] for x in (dl, dr) for n in range(12)], axis=1)
 
-    def send_back(k, carry):
-        q = (mine + k) % 128
-        remote(s4.at[q], r4.at[mine], 7, ((q % 8) * 4 + quarter, q // 8)).start()
-        return carry
-
-    lax.fori_loop(1, 128, send_back, 0)
+    def send_back(place, column):
+        remote(s4.at[column * 8 + place], r4.at[mine], 7, (place * 4 + quarter, column)).start()
+
+    each_channel(send_back)
     pltpu.make_async_copy(s4.at[mine], r4.at[mine], recv_sem.at[7]).start()
 
     wait(r4, recv_sem.at[7])
     dl = r4[:, 0, 0:288]
     dr = r4[:, 0, 288:576]
     stacked = jnp.concatenate([dl * keep[2], dl * keep[1], dr * keep[4], dr * keep[3]], axis=0)
-    weights = jnp.concatenate([gate_a_ref[...], proj_a_ref[...], gate_b_ref[...], proj_b_ref[...]], axis=1)
-    grad = (product(split(weights), split(stacked)) + keep[6]) * ng
+    grad = (product(split(weights_ref[:, 0:512]), split(stacked)) + keep[6]) * ng
     plain = keep[0]
     grad = stats[0:1] * (grad - mean0(grad) - plain * mean0(grad * plain))
     out_ref[...] = grad.T.reshape(12, 24, 128)
@@ -278,9 +306,10 @@
     return pl.pallas_call(
         kernel,
         out_shape=jax.ShapeDtypeStruct(pair.shape, F32),
-        in_specs=[pl.BlockSpec(memory_space=pltpu.VMEM)] * 10,
+        in_specs=[pl.BlockSpec(memory_space=pltpu.HBM)] * 10,
         out_specs=pl.BlockSpec(memory_space=pltpu.VMEM),
         scratch_shapes=[
+            vmem(12, 24, 128), vmem(12, 24, 128), vmem(2, 1, 128), vmem(128, 640), vmem(128, 128),
             vmem(128, 1, 576), vmem(128, 1, 576),
             vmem(2, 96, 384), vmem(2, 96, 384), vmem(3, 192, 128),
             vmem(128, 1, 288), vmem(128, 1, 288),
@@ -290,10 +319,10 @@
             vmem(3, 192, 128), vmem(2, 96, 384), vmem(96, 384),
             vmem(128, 1, 576), vmem(128, 1, 576),
             vmem(8, 128, 288), vmem(8, 288),
-            pltpu.SemaphoreType.DMA((8,)), pltpu.SemaphoreType.DMA((8,)), pltpu.SemaphoreType.REGULAR,
+            pltpu.SemaphoreType.DMA((10,)), pltpu.SemaphoreType.DMA((8,)), pltpu.SemaphoreType.DMA((8,)),
         ],
         compiler_params=pltpu.CompilerParams(
-            collective_id=0, has_side_effects=True, vmem_limit_bytes=48 * 1024 * 1024),
+            collective_id=0, has_side_effects=True, vmem_limit_bytes=64 * 1024 * 1024 - 65536),
     )(pair, cotangent, norm_gain.reshape(1, 128), gate_a, proj_a, gate_b, proj_b, mix_gain.reshape(1, 128),
       out_gate, out_proj)
 

time: 84.6 us -> 72.2 us (0.85)
  the two profiles are of different devices: /device:TPU:16 before, /device:TPU:2 now
where the time goes in v1:
time: 72.2 us; the launch traced here: 72.1 us
  Pallas kernels  70.5 us (98%)
  local copies, waits for them, and re-layouts  1.58 us (2%)
    pallas_call x1, Pallas kernels, local(): pl.pallas_call(kernel, out_shape=jax.ShapeDtypeStruct(pair.shape, F32), i...  70.5 us
    unnamed x1, local copies, waits for them, and re-layouts  1.58 us

profile of v1, /device:TPU:2, one launch (start us, length us, event | category | flops | bytes accessed | tf_op | source)
XLA Modules:
  0.0 72.1 jit_solution(11279581634645948305)
XLA Ops:
  0.0 70.5 %shard_map.100 = f32[12,24,128]{2,1,0:T(8,128)} custom-call(f32[12,24,128]{2,1,0:T(8,128)} %pair_hbm.1, f32[12,24,128]{2,1,0:T(8,128)} %cot_hbm.1, f32[1,128]{1,0:T(1,128)} %bitcast.2, f32[128,128]{1,0:T(8,128)} %gate_a_hbm.1, f32[128,128]{1,0:T(8,128)} %proj_a_hbm.1, f32[128,128]{1,0:T(8,128)} %gate_b_hbm.1, f32[128,128]{1,0:T(8,128)} %proj_b_hbm.1, ...), custom_call_target="tpu_custom_call" | custom-call | tf_op jit(solution)/shard_map/pallas_call | solution.py:306
  70.5 1.6 %copy.12 = f32[12,24,128]{2,1,0:T(8,128)} copy(f32[12,24,128]{2,1,0:T(8,128)} %shard_map.100) | data formatting | bytes 294912

commit v2 on v1

--- a/solution.py
+++ b/solution.py
@@ -5,6 +5,20 @@
 from jax.experimental.pallas import tpu as pltpu
 from jax.sharding import PartitionSpec as P
 
+
+def far_first(sizes, hops):
+    steps = [(y, z, x) for y in range(sizes[0]) for z in range(sizes[1]) for x in range(sizes[2])]
+    return sorted(steps, key=lambda s: (-hops(*s), (s[0] * 41 + s[1] * 23 + s[2] * 67 + s[0] * s[1] * 29) * 53 % 131))
+
+
+def ring(step):
+    return min(step, 8 - step)
+
+
+CHANNELS = far_first((8, 8, 2), lambda y, z, x: ring(y) + ring(z) + 2 * x)[:-1]
+SAME_X = far_first((8, 4, 2), lambda y, z, x: ring(y) + ring(2 * z) + 2 * x)[:-1]
+OTHER_X = far_first((8, 4, 2), lambda y, z, x: ring(y) + ring(2 * z))
+VMEM = 64 * 1024 * 1024 - 65536
 MESH = pl.DeviceIdType.MESH
 F32 = jnp.float32
 NN = (((1,), (0,)), ((), ()))
@@ -68,30 +82,16 @@
     def greet(device):
         pl.semaphore_signal(barrier, inc=1, device_id=device, device_id_type=MESH)
 
-    def mod(value, size):
-        return lax.rem(value, size)
-
     y_here, z_here = lax.div(col, 2), lax.div(row, 8) * 2 + lax.rem(col, 2)
-    z_all = [mod(z_here + t, 8) for t in range(8)]
+    y_column = [lax.rem(y_here + t, 8) * 2 for t in range(8)]
+    z_all = [lax.rem(z_here + t, 8) for t in range(8)]
     z_place = [lax.div(z, 2) * 2 for z in z_all]
     z_column = [lax.rem(z, 2) for z in z_all]
     x_place = [lax.rem(part + t, 2) for t in range(2)]
 
-    def y_far(step):
-        return mod(y_here + 4 + lax.div(step + 1, 2) * (1 - 2 * mod(step, 2)), 8) * 2
-
-    inner = sorted(((z, x) for z in range(8) for x in range(2)), key=lambda o: -min(o[0], 8 - o[0]) - 2 * o[1])
-
     def each_channel(visit):
-        def one(step, carry):
-            column = y_far(step)
-            for z, x in inner:
-                visit(z_place[z] + x_place[x], column + z_column[z])
-            return carry
-
-        lax.fori_loop(0, 7, one, 0)
-        for z, x in inner[:-1]:
-            visit(z_place[z] + x_place[x], y_here * 2 + z_column[z])
+        for y, z, x in CHANNELS:
+            visit(z_place[z] + x_place[x], y_column[y] + z_column[z])
 
     greet(x_peer)
     greet(core_peer)
@@ -184,22 +184,13 @@
                       (place * 4 + half * 2 + core, column + low))
 
     z_half = [lax.rem(lax.div(row, 8) + t, 4) * 2 for t in range(4)]
-    inner_half = ((2, 1), (2, 0), (1, 1), (3, 1), (1, 0), (3, 0), (0, 1), (0, 0))
-
-    def send_mixed(half, last):
-        def one(step, carry):
-            column = y_far(step)
-            for z, x in inner_half:
-                mixed_copy(half, column, z_half[z] + x_place[x]).start()
-            return carry
-
-        lax.fori_loop(0, 7, one, 0)
-        for z, x in inner_half[:last]:
-            mixed_copy(half, y_here * 2, z_half[z] + x_place[x]).start()
+    def send_mixed(half, steps):
+        for y, z, x in steps:
+            mixed_copy(half, y_column[y], z_half[z] + x_place[x]).start()
 
     mix(low)
 
-    send_mixed(low, 7)
+    send_mixed(low, SAME_X)
 
     @pl.when(same)
     def _():
@@ -207,12 +198,12 @@
 
     @pl.when(jnp.logical_not(same))
     def _():
-        mixed_copy(low, y_here * 2, part).start()
+        mixed_copy(low, y_column[0], part).start()
 
     send_left.wait_recv()
     mix(1 - low)
 
-    send_mixed(1 - low, 8)
+    send_mixed(1 - low, OTHER_X)
 
     wait(r2, recv_sem.at[3])
     mixed = r2[:, 0, :]
@@ -322,7 +313,7 @@
             pltpu.SemaphoreType.DMA((10,)), pltpu.SemaphoreType.DMA((8,)), pltpu.SemaphoreType.DMA((8,)),
         ],
         compiler_params=pltpu.CompilerParams(
-            collective_id=0, has_side_effects=True, vmem_limit_bytes=64 * 1024 * 1024 - 65536),
+            collective_id=0, has_side_effects=True, vmem_limit_bytes=VMEM),
     )(pair, cotangent, norm_gain.reshape(1, 128), gate_a, proj_a, gate_b, proj_b, mix_gain.reshape(1, 128),
       out_gate, out_proj)
 

time: 72.2 us -> 69 us (0.956)
  the two profiles are of different devices: /device:TPU:2 before, /device:TPU:8 now
where the time goes in v2:
time: 69 us; the launch traced here: 68.8 us
  Pallas kernels  67.2 us (97%)
  local copies, waits for them, and re-layouts  1.58 us (2%)
    pallas_call x1, Pallas kernels, local(): pl.pallas_call(kernel, out_shape=jax.ShapeDtypeStruct(pair.shape, F32), i...  67.2 us
    unnamed x1, local copies, waits for them, and re-layouts  1.58 us

profile of v2, /device:TPU:8, one launch (start us, length us, event | category | flops | bytes accessed | tf_op | source)
XLA Modules:
  0.0 68.8 jit_solution(2632032686419303192)
XLA Ops:
  0.0 67.2 %shard_map.100 = f32[12,24,128]{2,1,0:T(8,128)} custom-call(f32[12,24,128]{2,1,0:T(8,128)} %pair_hbm.1, f32[12,24,128]{2,1,0:T(8,128)} %cot_hbm.1, f32[1,128]{1,0:T(1,128)} %bitcast.2, f32[128,128]{1,0:T(8,128)} %gate_a_hbm.1, f32[128,128]{1,0:T(8,128)} %proj_a_hbm.1, f32[128,128]{1,0:T(8,128)} %gate_b_hbm.1, f32[128,128]{1,0:T(8,128)} %proj_b_hbm.1, ...), custom_call_target="tpu_custom_call" | custom-call | tf_op jit(solution)/shard_map/pallas_call | solution.py:297
  67.3 1.6 %copy.12 = f32[12,24,128]{2,1,0:T(8,128)} copy(f32[12,24,128]{2,1,0:T(8,128)} %shard_map.100) | data formatting | bytes 294912

commit v3 on v2

--- a/solution.py
+++ b/solution.py
@@ -1,3 +1,5 @@
+import random
+
 import jax
 import jax.numpy as jnp
 from jax import lax
@@ -8,7 +10,8 @@
 
 def far_first(sizes, hops):
     steps = [(y, z, x) for y in range(sizes[0]) for z in range(sizes[1]) for x in range(sizes[2])]
-    return sorted(steps, key=lambda s: (-hops(*s), (s[0] * 41 + s[1] * 23 + s[2] * 67 + s[0] * s[1] * 29) * 53 % 131))
+    random.Random(0).shuffle(steps)
+    return sorted(steps, key=lambda s: -hops(*s))
 
 
 def ring(step):
@@ -231,26 +234,35 @@
     out_value = product(split(out_proj.T), split(mixed_plain * mg))
     keep[6] = product(split(weights_ref[:, 512:640]), split(keep[5] * out_value))
 
-    wait(r3, recv_sem.at[4])
-    for half in range(2):
+    right = right_all()
+    left = split(left_x[...].reshape(192, 384))
+
+    def turn_grad(half):
         for n in range(12):
             grad_x[half, 8 * n:8 * n + 8, :] = jnp.concatenate(
-                [r3[64 * half + 8 * b:64 * half + 8 * b + 8, 0, 24 * n:24 * n + 24] for b in range(8)], axis=1)
-    right = right_all()
+                [r3[pl.ds(64 * half + 8 * b, 8), 0, 24 * n:24 * n + 24] for b in range(8)], axis=1)
+
+    wait(r3, recv_sem.at[4])
+    turn_grad(1 - low)
     dl_out[...] = product(split(grad_x[1 - low]), right)
     send_dl = remote(dl_out, dl_in, 5, x_peer)
     send_dl.start()
+    turn_grad(low)
     grad_t = grad_x[...].reshape(192, 192).T
-    dr = product(split(grad_t), split(left_x[...].reshape(192, 384)))
+    dr = product(split(grad_t), left)
     for t in range(3):
         dr_full[t] = dr[:, 128 * t:128 * t + 128]
-    for side in range(2):
+
+    def turn_rows(side):
         for n in range(12):
             for t in range(3):
                 dr_t[side, 8 * n:8 * n + 8, 128 * t:128 * t + 128] = dr_full[
                     t, pl.ds(12 * side + n, 8, stride=24), :]
+
+    turn_rows(1 - core)
     send_dr = remote(dr_t.at[1 - core], dr_in, 6, core_peer)
     send_dr.start()
+    turn_rows(core)
     dl_own[...] = product(split(grad_x[low]), right)
     send_dr.wait_recv()
     send_dl.wait_recv()
@@ -266,12 +278,14 @@
     each_channel(send_back)
     pltpu.make_async_copy(s4.at[mine], r4.at[mine], recv_sem.at[7]).start()
 
+    weights = split(weights_ref[:, 0:512])
+    plain = keep[0]
+    partial = keep[6]
     wait(r4, recv_sem.at[7])
     dl = r4[:, 0, 0:288]
     dr = r4[:, 0, 288:576]
     stacked = jnp.concatenate([dl * keep[2], dl * keep[1], dr * keep[4], dr * keep[3]], axis=0)
-    grad = (product(split(weights_ref[:, 0:512]), split(stacked)) + keep[6]) * ng
-    plain = keep[0]
+    grad = (product(weights, split(stacked)) + partial) * ng
     grad = stats[0:1] * (grad - mean0(grad) - plain * mean0(grad * plain))
     out_ref[...] = grad.T.reshape(12, 24, 128)
 

time: 69 us -> 68.4 us (level)
  no operation moved by 1% of the time
where the time goes in v3:
time: 68.4 us; the launch traced here: 68.2 us
  Pallas kernels  66.6 us (97%)
  local copies, waits for them, and re-layouts  1.58 us (2%)
    pallas_call x1, Pallas kernels, local(): pl.pallas_call(kernel, out_shape=jax.ShapeDtypeStruct(pair.shape, F32), i...  66.6 us
    unnamed x1, local copies, waits for them, and re-layouts  1.58 us

profile of v3, /device:TPU:8, one launch (start us, length us, event | category | flops | bytes accessed | tf_op | source)
XLA Modules:
  0.0 68.2 jit_solution(9992475527465908864)
XLA Ops:
  0.0 66.6 %shard_map.100 = f32[12,24,128]{2,1,0:T(8,128)} custom-call(f32[12,24,128]{2,1,0:T(8,128)} %pair_hbm.1, f32[12,24,128]{2,1,0:T(8,128)} %cot_hbm.1, f32[1,128]{1,0:T(1,128)} %bitcast.2, f32[128,128]{1,0:T(8,128)} %gate_a_hbm.1, f32[128,128]{1,0:T(8,128)} %proj_a_hbm.1, f32[128,128]{1,0:T(8,128)} %gate_b_hbm.1, f32[128,128]{1,0:T(8,128)} %proj_b_hbm.1, ...), custom_call_target="tpu_custom_call" | custom-call | tf_op jit(solution)/shard_map/pallas_call | solution.py:311
  66.6 1.6 %copy.12 = f32[12,24,128]{2,1,0:T(8,128)} copy(f32[12,24,128]{2,1,0:T(8,128)} %shard_map.100) | data formatting | bytes 294912
